TPU v7x, 256 devices: a whole 4x4x8 slice. The times are simulated.
256 devices in a mesh: replica: 16 (over x_lo, z), outer: 16 (over x_hi, y, core).
Axes of the slice: x: 4 (x_hi: 2, x_lo: 2; x = x_hi * 2 + x_lo), y: 4, z: 8, core: 2. Of those that a mesh axis runs over, the one named last changes fastest.
Arguments:
- tokens: bfloat16 [32768, 14848], P(('replica', 'outer')), may hold values from -24 to 24
- cotangent: bfloat16 [32768, 1024], P(('replica', 'outer')), may hold values from -3 to 3
- kv_weight: bfloat16 [14848, 1024], P('outer'), may hold values from -0.046875 to 0.046875
- gain: float32 [14848], replicated, may hold values from 0.25 to 2
- bias: float32 [14848], replicated, may hold values from -4 to 4
Outputs:
- grad_tokens: bfloat16 [32768, 14848], P(('replica', 'outer'))
- grad_weight: bfloat16 [14848, 1024], P('outer')
- grad_gain: float32 [14848], replicated
- grad_bias: float32 [14848], replicated
All inputs are finite; a program needn't handle non-finite values.
Results may differ from a plain program's by a relative error of at most 0.0049.
Values may be sent and summed in bfloat16 or wider, within the bound.
A program may use at most 256 MiB of HBM per device.

v0:
```python
import jax
import jax.numpy as jnp
from jax import lax
from jax.sharding import PartitionSpec as P

epsilon = 1e-05


def layer_stats(rows):
    values = rows.astype(jnp.float32)
    centre_mean = jnp.mean(values, axis=1, keepdims=True)
    centre = values - centre_mean
    inv_std = lax.rsqrt(jnp.mean(centre * centre, axis=1, keepdims=True) + epsilon)
    return (centre * inv_std, inv_std, centre_mean)


def norm_backward(grad_hidden, normed, inv_std, gain):
    scaled = gain[None, :] * lax.optimization_barrier(grad_hidden).astype(jnp.float32)
    first = jnp.mean(scaled, axis=1, keepdims=True)
    second = jnp.mean(scaled * normed, axis=1, keepdims=True)
    return (inv_std * (scaled - first - normed * second)).astype(jnp.bfloat16)


def body(tokens, cotangent, kv_weight, gain, bias):
    width = gain.shape[0]
    share = kv_weight.shape[0]
    replicas = lax.axis_size("replica")
    normed, inv_std, centre_mean = layer_stats(tokens)
    feature_cols = lax.all_to_all(tokens, "outer", split_axis=1, concat_axis=0, tiled=True)
    gathered = (
        lax.all_gather(cotangent.astype(jnp.float32), "outer", axis=0, tiled=True),
        lax.all_gather(centre_mean[:, 0], "outer", axis=0, tiled=True),
        lax.all_gather(inv_std[:, 0], "outer", axis=0, tiled=True),
    )
    cot_all = gathered[0].astype(jnp.bfloat16)
    offset = lax.axis_index("outer") * share
    gain_cols = lax.dynamic_slice_in_dim(gain, offset, share, 0)
    bias_cols = lax.dynamic_slice_in_dim(bias, offset, share, 0)
    normed_cols = (feature_cols.astype(jnp.float32) - gathered[1][:, None]) * gathered[2][:, None]
    hidden_cols = (gain_cols[None, :] * normed_cols + bias_cols[None, :]).astype(jnp.bfloat16)
    grad_cols = lax.dot_general(
        cot_all, kv_weight, (((1,), (1,)), ((), ())), preferred_element_type=jnp.float32
    ).astype(jnp.bfloat16)
    shard_weight = lax.dot_general(
        hidden_cols, cot_all, (((0,), (0,)), ((), ())), preferred_element_type=jnp.float32
    )
    grad_cols_float = lax.optimization_barrier(grad_cols).astype(jnp.float32)
    gain_part = lax.dynamic_update_slice(
        jnp.zeros((width,), jnp.float32), jnp.sum(grad_cols_float * normed_cols, axis=0), (offset,)
    )
    bias_part = lax.dynamic_update_slice(
        jnp.zeros((width,), jnp.float32), jnp.sum(grad_cols_float, axis=0), (offset,)
    )
    grad_hidden = lax.all_to_all(grad_cols, "outer", split_axis=0, concat_axis=1, tiled=True)
    shard_weight = (lax.psum(shard_weight, "replica") / replicas).astype(jnp.bfloat16)
    gain_total, bias_total = lax.psum((gain_part, bias_part), ("replica", "outer"))
    grad_tokens = norm_backward(grad_hidden, normed, inv_std, gain)
    return (grad_tokens, shard_weight, gain_total / replicas, bias_total / replicas)


def solution(mesh):
    in_specs = (
        P(("replica", "outer"), None),
        P(("replica", "outer"), None),
        P("outer", None),
        P(),
        P(),
    )
    out_specs = (P(("replica", "outer"), None), P("outer", None), P(), P())
    return jax.shard_map(body, mesh=mesh, in_specs=in_specs, out_specs=out_specs, check_vma=False)
```

profile of v0, /device:TPU:1, one launch (start us, length us, event | category | flops | bytes accessed | tf_op | source)
XLA Modules:
  0.0 601.8 jit_solution(18020737409192248317)
XLA Ops:
  7.2 0.0 all-gather.4.cloned.1.call-start
  7.2 0.7 all-gather.4.cloned.1.call-update
  7.9 6.1 %copy.16 = bf16[128,14848]{0,1:T(8,128)(2,1)} copy(bf16[128,14848]{1,0:T(8,128)(2,1)} %param.5) | data formatting | bytes 7602176 | tf_op args[0]
  14.0 8.4 %all-to-all-start.1 = ((bf16[128,16,928]{0,2,1:T(8,128)(2,1)}), bf16[128,16,928]{0,2,1:T(8,128)(2,1)}, u32[]{:S(2)}, u32[]{:S(2)}) async-start(bf16[128,16,928]{0,2,1:T(8,128)(2,1)} %bitcast.33), calls=%async_computation.1 | async-start | bytes 7602176 | tf_op jit(solution)/shard_map/all_to_all | solution.py:29
  22.5 79.6 %all-gather.4.cloned.1.call-done = bf16[2048,1024]{1,0:T(8,128)(2,1)} async-done(((bf16[128,1024]{1,0:T(8,128)(2,1)}), bf16[2048,1024]{1,0:T(8,128)(2,1)}) %all-gather.4.cloned.1.call-update) | async-done | bytes 4194320 | tf_op jit(solution)/shard_map/all_gather | solution.py:31
  102.0 6.5 %convolution_convert_fusion = bf16[2048,928]{0,1:T(8,128)(2,1)S(1)} fusion(bf16[928,1024]{1,0:T(8,128)(2,1)S(1)} %copy-done, bf16[2048,1024]{1,0:T(8,128)(2,1)} %all-gather.4.cloned.1.call-done), kind=kOutput, calls=%fused_computation.27 | convolution fusion | flops 3894214656 | bytes 9895936 | tf_op jit(solution)/shard_map/dot_general | solution.py:41
  108.6 1.9 copy-done.3
  110.5 2.6 copy_bitcast_fusion
  113.1 4.6 all-to-all-start
  117.7 0.0 all-reduce.6.cloned.1.call-start
  117.8 0.9 dynamic_slice.7
  118.7 0.1 dynamic_slice.6
  118.8 4.0 convert_reduce_fusion.1
  122.8 2.0 fusion.8
  124.8 59.4 %all-gather.1 = f32[16,1,128]{2,1,0:T(1,128)S(1)} all-gather(f32[1,1,128]{2,1,0:T(1,128)S(1)} %get-tuple-element.20), channel_id=1, replica_groups=mesh['replica'=16,'outer'=16] {'outer'}, dimensions={0}, use_global_device_ids=true | all-gather | bytes 8704 | tf_op jit(solution)/shard_map/all_gather | solution.py:33
  184.3 19.1 %all-gather = f32[16,1,128]{2,1,0:T(1,128)S(1)} all-gather(f32[1,1,128]{2,1,0:T(1,128)S(1)} %get-tuple-element.18), channel_id=1, replica_groups=mesh['replica'=16,'outer'=16] {'outer'}, dimensions={0}, use_global_device_ids=true | all-gather | bytes 8704 | tf_op jit(solution)/shard_map/all_gather | solution.py:32
  203.4 3.9 convert_reduce_fusion
  207.3 0.3 dynamic_update_slice.6
  207.6 0.3 dynamic_update_slice.7
  207.9 0.3 copy-done.7
  208.2 0.3 copy-done.6
  208.5 0.0 all-reduce.6.cloned.1.call-update
  208.5 0.2 all-reduce.4.cloned.1.call-start
  208.8 9.4 %fusion.12 = f32[928,1024]{1,0:T(8,128)} fusion(f32[928]{0:T(1024)S(1)} %dynamic_slice.7, f32[2048]{0:T(1024)S(1)} %bitcast.35, f32[2048]{0:T(1024)S(1)} %bitcast.37, f32[928]{0:T(1024)S(1)} %dynamic_slice.6, bf16[2048,1024]{1,0:T(8,128)(2,1)} %all-gather.4.cloned.1.call-done, bf16[128,16,928]{0,2,1:T(8,128)(2,1)} %all-to-all-done.1), kind=kOutput, calls=%fused_computation.20 | convolution fusion | flops 3903717376 | bytes 11820288 | tf_op jit(solution)/shard_map/dot_general | solution.py:44
  218.2 0.0 all-reduce.4.cloned.1.call-update
  218.2 230.3 %all-reduce.6.cloned.1.call-done = (f32[14848]{0:T(1024)}, f32[14848]{0:T(1024)}) async-done(((f32[14848]{0:T(1024)}, f32[14848]{0:T(1024)}), (f32[14848]{0:T(1024)}, f32[14848]{0:T(1024)})) %all-reduce.6.cloned.1.call-update) | async-done | bytes 118800 | tf_op jit(solution)/shard_map/psum | solution.py:56
  448.5 1.5 broadcast_multiply_fusion
  450.0 8.0 %fusion.11 = (f32[128]{0:T(128)S(1)}, f32[128]{0:T(128)S(1)}) fusion(bf16[128,14848]{0,1:T(8,128)(2,1)} %bitcast.1, f32[14848]{0:T(1024)S(1)} %copy-done.5, f32[128]{0:T(128)S(1)} %get-tuple-element.21, f32[128]{0:T(128)S(1)} %get-tuple-element.19, bf16[128,14848]{0,1:T(8,128)(2,1)} %copy.16), kind=kLoop, calls=%fused_computation.19 | loop fusion | flops 15204096 | bytes 7663616 | tf_op jit(solution)/shard_map/reduce_sum | solution.py:19
  458.0 8.5 %fusion.7 = bf16[128,14848]{0,1:T(8,128)(2,1)} fusion(bf16[128,14848]{0,1:T(8,128)(2,1)S(1)} %copy-done.2, bf16[128,14848]{0,1:T(8,128)(2,1)} %bitcast.1, f32[128]{0:T(128)S(1)} %get-tuple-element.22, f32[128]{0:T(128)S(1)} %get-tuple-element.23, f32[14848]{0:T(1024)S(1)} %copy-done.5, f32[128]{0:T(128)S(1)} %get-tuple-element.21, f32[128]{0:T(128)S(1)} %get-tuple-element.19), kind=kLoop, calls=%fused_computation.11 | loop fusion | flops 19005440 | bytes 11464704 | tf_op jit(solution)/shard_map/convert_element_type | solution.py:21
  466.5 6.1 %copy.20 = bf16[128,14848]{1,0:T(8,128)(2,1)} copy(bf16[128,14848]{0,1:T(8,128)(2,1)} %fusion.7) | data formatting | bytes 7602176
  472.6 118.8 %all-reduce.4.cloned.1.call-done = f32[928,1024]{1,0:T(8,128)} async-done(((f32[928,1024]{1,0:T(8,128)}), f32[928,1024]{1,0:T(8,128)}) %all-reduce.4.cloned.1.call-update) | async-done | bytes 3801104 | tf_op jit(solution)/shard_map/psum | solution.py:55
  591.4 3.8 multiply_convert_fusion
  (20 shorter events, 0.1 us)
Async XLA Ops:
  7.2 94.9 %copy-start = (bf16[928,1024]{1,0:T(8,128)(2,1)S(1)}, bf16[928,1024]{1,0:T(8,128)(2,1)}, u32[]{:S(2)}) copy-start(bf16[928,1024]{1,0:T(8,128)(2,1)} %param.7) | copy-start | bytes 5701636
  7.2 94.9 %all-gather.4.cloned.1.call-start = ((), (), s32[]{:S(2)}) async-start(), calls=%async_computation.2 | async-start | bytes 4456448 | tf_op jit(solution)/shard_map/all_gather | solution.py:31
  14.0 99.1 %all-to-all-start.1 = ((bf16[128,16,928]{0,2,1:T(8,128)(2,1)}), bf16[128,16,928]{0,2,1:T(8,128)(2,1)}, u32[]{:S(2)}, u32[]{:S(2)}) async-start(bf16[128,16,928]{0,2,1:T(8,128)(2,1)} %bitcast.33), calls=%async_computation.1 | async-start | bytes 7602176 | tf_op jit(solution)/shard_map/all_to_all | solution.py:29
  108.6 1.9 copy-start.3
  113.1 5.6 copy-start.5
  113.1 336.9 %all-to-all-start = ((bf16[16,128,928]{1,2,0:T(8,128)(2,1)}), bf16[16,128,928]{1,2,0:T(8,128)(2,1)}, u32[]{:S(2)}, u32[]{:S(2)}) async-start(bf16[16,128,928]{1,2,0:T(8,128)(2,1)} %copy_bitcast_fusion), calls=%async_computation | async-start | bytes 7602176 | tf_op jit(solution)/shard_map/all_to_all | solution.py:54
  117.7 330.8 %all-reduce.6.cloned.1.call-start = ((), (), s32[]{:S(2)}) async-start(), calls=%async_computation.4 | async-start | bytes 245760 | tf_op jit(solution)/shard_map/psum | solution.py:56
  117.8 5.0 copy-start.1
  117.8 85.6 %copy-start.4 = (bf16[2048,928]{0,1:T(8,128)(2,1)S(1)}, bf16[2048,928]{0,1:T(8,128)(2,1)}, u32[]{:S(2)}) copy-start(bf16[2048,928]{0,1:T(8,128)(2,1)} %copy-done.3) | copy-start | bytes 11403268
  207.6 0.6 copy-start.7
  207.9 0.6 copy-start.6
  208.5 382.9 %all-reduce.4.cloned.1.call-start = ((), (), s32[]{:S(2)}) async-start(), calls=%async_computation.3 | async-start | bytes 7602176 | tf_op jit(solution)/shard_map/psum | solution.py:55
  450.0 8.0 %copy-start.2 = (bf16[128,14848]{0,1:T(8,128)(2,1)S(1)}, bf16[128,14848]{0,1:T(8,128)(2,1)}, u32[]{:S(2)}) copy-start(bf16[128,14848]{0,1:T(8,128)(2,1)} %copy.16) | copy-start | bytes 11403268
Sparse Core Ops, SparseCore 0:
  10.8 91.2 all-gather.3
  208.6 239.7 all-reduce.5
  451.2 140.1 all-reduce.3
where the time goes:
time: 611 us; the launch traced here: 602 us
  waiting for transfers between devices  429 us (70%)
  blocking collectives  78.5 us (13%)
  other arithmetic  31.8 us (5%)
  local copies, waits for them, and re-layouts  19 us (3%)
  matrix products  15.9 us (3%)
  between operations  13.8 us (2%)
  starting transfers between devices  13.4 us (2%)
    psum x1, waiting for transfers between devices, body(): lax.psum((gain_part, bias_part), ('replica', 'outer'))  230 us
    psum x1, waiting for transfers between devices, body(): lax.psum(shard_weight, 'replica') / replicas  119 us
    all_gather x1, waiting for transfers between devices, body(): lax.all_gather(cotangent.astype(jnp.float32), 'outer', axis=0, tiled=True)  79.6 us
    all_gather x1, blocking collectives, body(): lax.all_gather(inv_std[:, 0], 'outer', axis=0, tiled=True)  59.4 us
    all_gather x1, blocking collectives, body(): lax.all_gather(centre_mean[:, 0], 'outer', axis=0, tiled=True)  19.1 us
    unnamed x18, local copies, waits for them, and re-layouts  14.8 us
  transfers between devices with their start and end apart: 5, of which 3 were waited for; matrix products, arithmetic and copies ran while one was open for 10% of the time, Pallas kernels for 0%

commit v1 on v0

v1 whole, which is shorter than its diff:
```python
import jax
import jax.numpy as jnp
from jax import lax
from jax.experimental import pallas as pl
from jax.experimental.pallas import tpu as pltpu
from jax.sharding import PartitionSpec as P

BF = jnp.bfloat16
F32 = jnp.float32
MESH = pl.DeviceIdType.MESH
EPS = 1e-05

D = 14848
TOK = 128
KVW = 1024
N = 16
SH = D // N
RA = 480
RB = SH - RA
HALF = {0: RA // 2, 1: RB // 2}
BASE = {0: 0, 1: RA}
SIZE = {0: RA, 1: RB}


def div(a, b):
    return lax.div(a, jnp.int32(b))


def rem(a, b):
    return lax.rem(a, jnp.int32(b))


def kernel(x, cot, w, gain, bias, out, gw, gb,
           xT, tok, cots, stat, stats, hid, ghs, ghT, s_a, s_b, xr_a, xr_b,
           zs_a, zs_b, zr_a, zr_b, fin_a, fin_b, gcol, bcol, acc, gg, ggs, gtot,
           c_s, c_r, ta_s, ta_r, tb_s, tb_r, st_s, st_r, h_s, h_r,
           x_s, x_r, za_s, za_r, zb_s, zb_r, fa_s, fa_r, fb_s, fb_r, g_s, g_r, t_s, t_r, l_s):
    r = lax.axis_index("replica")
    o = lax.axis_index("outer")
    xlo, z = div(r, 8), rem(r, 8)
    xhi, y, c = div(o, 8), rem(div(o, 2), 4), rem(o, 2)

    def member(k, sign):
        dxh, dy, dc = div(k, 8), rem(div(k, 2), 4), rem(k, 2)
        xh = rem(xhi + dxh, 2)
        yy = rem(y + 4 + sign * dy, 4)
        cc = rem(c + dc, 2)
        xl = rem(xlo + dxh, 2)
        return xl * 8 + z, xh * 8 + yy * 2 + cc

    def ahead(k):
        return member(k, 1)

    def behind(k):
        return member(k, -1)

    def replica(k, sign):
        return rem(xlo + div(k, 8), 2) * 8 + rem(z + 8 + sign * rem(k, 8), 8), o

    bar = pltpu.get_barrier_semaphore()

    @pl.loop(1, N)
    def _(k):
        pl.semaphore_signal(bar, inc=1, device_id=ahead(k), device_id_type=MESH)
        pl.semaphore_signal(bar, inc=1, device_id=replica(k, 1), device_id_type=MESH)

    pl.semaphore_wait(bar, 2 * (N - 1))

    def remote(src, dst, ss, rs, dev):
        return pltpu.make_async_remote_copy(
            src_ref=src, dst_ref=dst, send_sem=ss, recv_sem=rs, device_id=dev, device_id_type=MESH)

    def rows(k, n=TOK):
        return pl.ds(pl.multiple_of(k * n, n), n)

    def cot_copy(k):
        return remote(cot, cots.at[rows(k)], c_s.at[k], c_r.at[k], ahead(k))

    def cot_forward(k):
        return remote(cots.at[rows(k)], cots.at[rows(k + 1)], c_s.at[k + 1], c_r.at[k + 1], ahead(jnp.int32(1)))

    own_cot = pltpu.make_async_copy(cot, cots.at[pl.ds(0, TOK)], l_s.at[0])
    own_cot.start()
    cot_copy(jnp.int32(1)).start()

    @pl.loop(1, 8)
    def _(j):
        cot_copy(2 * j).start()

    def turn(t, total):
        s = pl.multiple_of(t * 512, 512)
        v = x[:, pl.ds(s, 512)].T
        xT[pl.ds(s, 512), :] = v
        return total + v.astype(F32).reshape(64, 8, TOK).sum(0)

    total = lax.fori_loop(0, D // 512, turn, jnp.zeros((8, TOK), F32))
    mean = total.sum(0, keepdims=True) / D

    def tok_copy(k, part):
        ss, rs = (ta_s, ta_r) if part == 0 else (tb_s, tb_r)
        dev = ahead(k)
        at = pl.multiple_of(dev[1] * SH + BASE[part], 16)
        return remote(xT.at[pl.ds(at, SIZE[part])], tok.at[k, pl.ds(BASE[part], SIZE[part])],
                      ss.at[k], rs.at[k], dev)

    own_tok = pltpu.make_async_copy(xT.at[rows(o, SH)], tok.at[0], l_s.at[1])
    own_tok.start()
    for part in (0, 1):
        @pl.loop(1, N)
        def _(k):
            tok_copy(k, part).start()

    def spread(t, total):
        s = pl.multiple_of(t * 512, 512)
        v = xT[pl.ds(s, 512), :].astype(F32) - mean
        return total + (v * v).reshape(64, 8, TOK).sum(0)

    total = lax.fori_loop(0, D // 512, spread, jnp.zeros((8, TOK), F32))
    inv = lax.rsqrt(total.sum(0, keepdims=True) / D + EPS)
    stat[0:1, :] = mean
    stat[1:2, :] = inv
    stats[0, 0:1, :] = mean
    stats[0, 1:2, :] = inv

    def stat_copy(k):
        return remote(stat, stats.at[k], st_s.at[k], st_r.at[k], ahead(k))

    @pl.loop(1, N)
    def _(k):
        stat_copy(k).start()

    first_tile = pl.multiple_of(div(o * SH, 128) * 128, 128)
    shift = pl.multiple_of(rem(o, 4) * 32, 32)
    gcol[...] = jnp.broadcast_to(gain[:, pl.ds(first_tile, 1024)], (TOK, 1024)).T
    bcol[...] = jnp.broadcast_to(bias[:, pl.ds(first_tile, 1024)], (TOK, 1024)).T

    @pl.loop(1, 8)
    def _(j):
        cot_copy(2 * j).wait_recv()
        cot_forward(2 * j).start()

    own_cot.wait()

    @pl.loop(0, 8)
    def _(j):
        @pl.when(j == 0)
        def _():
            cot_copy(jnp.int32(1)).wait_recv()

        @pl.when(j > 0)
        def _():
            cot_forward(2 * j).wait_recv()

        v = lax.dot_general(w[...], cots[rows(j, 2 * TOK), :], (((1,), (1,)), ((), ())),
                            preferred_element_type=F32).astype(BF)
        ghs[2 * j] = v[:, :TOK]
        ghs[2 * j + 1] = v[:, TOK:]

    own_tok.wait()
    acc[...] = jnp.zeros_like(acc)

    def gh_copy(k):
        return remote(ghs.at[k], ghT.at[rows(o, SH)], h_s.at[k], h_r.at[k], behind(k))

    other = (rem(xlo + 1, 2) * 8 + z, o)

    def half_copy(part):
        s, xr = (s_a, xr_a) if part == 0 else (s_b, xr_b)
        h = HALF[part]
        return remote(s.at[:, pl.ds(pl.multiple_of((1 - xlo) * h, 16), h)], xr, x_s.at[part], x_r.at[part], other)

    for part in (0, 1):
        base, size = BASE[part], SIZE[part]
        s = (s_a, s_b)[part]

        @pl.loop(0, N)
        def _(k):
            @pl.when(k > 0)
            def _():
                tok_copy(k, part).wait_recv()
                if part == 0:
                    stat_copy(k).wait_recv()
            v = tok[k, base:base + size, :].astype(F32)
            normed = (v - stats[k, 0:1, :]) * stats[k, 1:2, :]
            at = pl.multiple_of(shift + base, 32)
            hid[0:size, rows(k)] = (gcol[pl.ds(at, size), :] * normed + bcol[pl.ds(at, size), :]).astype(BF)
            gh = ghs[k, base:base + size, :].astype(F32)
            acc[0, base:base + size, :] += gh * normed
            acc[1, base:base + size, :] += gh

        @pl.loop(0, 4)
        def _(n):
            v = jnp.dot(hid[0:size, :], cots[:, rows(n, 256)], preferred_element_type=F32).astype(BF)
            s[2 * n] = v[:, :128]
            s[2 * n + 1] = v[:, 128:]

        half_copy(part).start()
        if part == 0:
            own_gh = pltpu.make_async_copy(ghs.at[0], ghT.at[rows(o, SH)], l_s.at[2])
            own_gh.start()

            @pl.loop(1, N)
            def _(k):
                gh_copy(k).start()

    for i in (0, 1):
        for t in range(8):
            n = min(128, SH - t * 128)
            v = acc[i, t * 128:t * 128 + n, :].T.sum(0, keepdims=True)
            gg[i * 8 + t:i * 8 + t + 1, 0:n] = v
            if n < 128:
                gg[i * 8 + t:i * 8 + t + 1, n:128] = jnp.zeros((1, 128 - n), F32)

    def gg_copy(k):
        return remote(gg, ggs.at[r], g_s.at[k], g_r.at[k], replica(k, 1))

    ggs[r] = gg[...]

    @pl.loop(1, N)
    def _(k):
        gg_copy(k).start()

    def z_copy(part, k):
        zs, zr, ss, rs = ((zs_a, zr_a, za_s, za_r), (zs_b, zr_b, zb_s, zb_r))[part]
        dev = replica(k, 1)
        return remote(zs.at[rem(z + k, 8)], zr.at[k], ss.at[k], rs.at[k], dev)

    for part in (0, 1):
        s, xr, zs, zr = ((s_a, xr_a, zs_a, zr_a), (s_b, xr_b, zs_b, zr_b))[part]
        h = HALF[part]
        half_copy(part).wait_recv()
        mine = pl.multiple_of(xlo * h, 16)
        zs[...] = (s[:, pl.ds(mine, h), :].astype(F32) + xr[...].astype(F32)).astype(BF)

        @pl.loop(1, 8)
        def _(k):
            z_copy(part, k).start()

    def fin_copy(part, k):
        fin, ss, rs = ((fin_a, fa_s, fa_r), (fin_b, fb_s, fb_r))[part]
        h = HALF[part]
        at = pl.multiple_of(BASE[part] + xlo * h, 16)
        return remote(fin, gw.at[pl.ds(at, h), rows(z)], ss.at[k], rs.at[k], replica(k, 1))

    @pl.loop(1, N)
    def _(k):
        gg_copy(k).wait_recv()

    gtot[...] = ggs[...].sum(0) / N
    gb[o] = gtot[...]

    def gt_copy(k):
        return remote(gtot, gb.at[o], t_s.at[k], t_r.at[k], ahead(k))

    @pl.loop(1, N)
    def _(k):
        gt_copy(k).start()

    for part in (0, 1):
        s, xr, zs, zr, fin = ((s_a, xr_a, zs_a, zr_a, fin_a), (s_b, xr_b, zs_b, zr_b, fin_b))[part]
        h = HALF[part]

        @pl.loop(1, 8)
        def _(k):
            z_copy(part, k).wait_recv()

        mine = pl.multiple_of(xlo * h, 16)
        v = s[z, pl.ds(mine, h), :].astype(F32) + xr[z].astype(F32)
        for k in range(1, 8):
            v = v + zr[k].astype(F32)
        fin[...] = (v / N).astype(BF)
        gw[pl.ds(pl.multiple_of(BASE[part] + mine, 16), h), rows(z)] = fin[...]

        @pl.loop(1, N)
        def _(k):
            fin_copy(part, k).start()

    stat_t = jnp.broadcast_to(stat[0:1, :], (TOK, TOK)).T
    inv_t = jnp.broadcast_to(stat[1:2, :], (TOK, TOK)).T
    own_gh.wait()

    def piece(s, n, sums):
        g = ghT[pl.ds(s, n), :].T
        out[:, pl.ds(s, n)] = g
        a, b = sums
        for t in range(n // 128):
            at = pl.multiple_of(s + t * 128, 128)
            scaled = g[:, t * 128:t * 128 + 128].astype(F32) * gain[:, pl.ds(at, 128)]
            normed = (x[:, pl.ds(at, 128)].astype(F32) - stat_t) * inv_t
            a = a + scaled
            b = b + scaled * normed
        return a, b

    quarter = 2 * xhi + div(y, 2)
    sums = (jnp.zeros((TOK, TOK), F32), jnp.zeros((TOK, TOK), F32))

    def quarter_step(q, sums):
        qq = rem(quarter + q, 4)
        for m in range(4):
            po = qq * 4 + m
            pxh, py, pc = div(po, 8), rem(div(po, 2), 4), rem(po, 2)
            k = rem(pxh + xhi, 2) * 8 + rem(py + 4 - y, 4) * 2 + rem(pc + c, 2)

            @pl.when(k > 0)
            def _():
                gh_copy(k).wait_recv()

        start = qq * 3712

        def inner(t, sums):
            return piece(pl.multiple_of(start + t * 512, 128), 512, sums)

        sums = lax.fori_loop(0, 7, inner, sums)
        return piece(pl.multiple_of(start + 3584, 128), 128, sums)

    sums = lax.fori_loop(0, 4, quarter_step, sums)
    first = jnp.broadcast_to(sums[0].sum(1, keepdims=True) / D, (TOK, TOK))
    second = jnp.broadcast_to(sums[1].sum(1, keepdims=True) / D, (TOK, TOK))

    @pl.loop(0, D // 512)
    def _(t):
        for u in range(4):
            at = pl.multiple_of(t * 512 + u * 128, 128)
            scaled = out[:, pl.ds(at, 128)].astype(F32) * gain[:, pl.ds(at, 128)]
            normed = (x[:, pl.ds(at, 128)].astype(F32) - stat_t) * inv_t
            out[:, pl.ds(at, 128)] = (inv_t * (scaled - first - normed * second)).astype(BF)

    @pl.loop(1, N)
    def _(k):
        fin_copy(0, k).wait_recv()
        fin_copy(1, k).wait_recv()
        gt_copy(k).wait_recv()

    @pl.loop(1, N)
    def _(k):
        tok_copy(k, 0).wait_send()
        tok_copy(k, 1).wait_send()
        stat_copy(k).wait_send()
        gh_copy(k).wait_send()
        gg_copy(k).wait_send()
        gt_copy(k).wait_send()
        fin_copy(0, k).wait_send()
        fin_copy(1, k).wait_send()

    cot_copy(jnp.int32(1)).wait_send()

    @pl.loop(1, 8)
    def _(j):
        cot_copy(2 * j).wait_send()
        cot_forward(2 * j).wait_send()
        z_copy(0, j).wait_send()
        z_copy(1, j).wait_send()

    half_copy(0).wait_send()
    half_copy(1).wait_send()


def body(tokens, cotangent, kv_weight, gain, bias):
    V = pl.BlockSpec(memory_space=pltpu.VMEM)
    ha, hb = HALF[0], HALF[1]
    scratch = [
        pltpu.VMEM((D, TOK), BF),
        pltpu.VMEM((N, SH, TOK), BF),
        pltpu.VMEM((N * TOK, KVW), BF),
        pltpu.VMEM((8, TOK), F32),
        pltpu.VMEM((N, 8, TOK), F32),
        pltpu.VMEM((RA, N * TOK), BF),
        pltpu.VMEM((N, SH, TOK), BF),
        pltpu.VMEM((D, TOK), BF),
        pltpu.VMEM((8, RA, 128), BF),
        pltpu.VMEM((8, RB, 128), BF),
        pltpu.VMEM((8, ha, 128), BF),
        pltpu.VMEM((8, hb, 128), BF),
        pltpu.VMEM((8, ha, 128), BF),
        pltpu.VMEM((8, hb, 128), BF),
        pltpu.VMEM((8, ha, 128), BF),
        pltpu.VMEM((8, hb, 128), BF),
        pltpu.VMEM((ha, 128), BF),
        pltpu.VMEM((hb, 128), BF),
        pltpu.VMEM((1024, TOK), F32),
        pltpu.VMEM((1024, TOK), F32),
        pltpu.VMEM((2, SH, TOK), F32),
        pltpu.VMEM((N, 128), F32),
        pltpu.VMEM((N, N, 128), F32),
        pltpu.VMEM((N, 128), F32),
    ]
    dma = pltpu.SemaphoreType.DMA
    sems = [dma((N,))] * 10 + [dma((2,))] * 2 + [dma((8,))] * 4 + [dma((N,))] * 8 + [dma((3,))]
    out, gw, gb = pl.pallas_call(
        kernel,
        out_shape=(
            jax.ShapeDtypeStruct((TOK, D), BF),
            jax.ShapeDtypeStruct((SH, KVW), BF),
            jax.ShapeDtypeStruct((N, N, 128), F32),
        ),
        in_specs=[V] * 5,
        out_specs=(V, V, V),
        scratch_shapes=scratch + sems,
        compiler_params=pltpu.CompilerParams(
            collective_id=0, has_side_effects=True, vmem_limit_bytes=60 << 20),
    )(tokens, cotangent, kv_weight, gain.reshape(1, D), bias.reshape(1, D))
    gb = gb.reshape(N, 2, 1024)[:, :, :SH]
    return out, gw, gb[:, 0].reshape(D), gb[:, 1].reshape(D)


def solution(mesh):
    in_specs = (
        P(("replica", "outer"), None),
        P(("replica", "outer"), None),
        P("outer", None),
        P(),
        P(),
    )
    out_specs = (P(("replica", "outer"), None), P("outer", None), P(), P())
    return jax.shard_map(body, mesh=mesh, in_specs=in_specs, out_specs=out_specs, check_vma=False)
```

time: 611 us -> 181 us (0.30); the launches traced: 602 us -> 180 us
  waiting for transfers between devices: 429 us -> 0 us
  Pallas kernels: 0 us -> 168 us
  blocking collectives: 78.5 us -> 0 us
  other arithmetic: 31.8 us -> 0 us
  matrix products: 15.9 us -> 0 us
  starting transfers between devices: 13.4 us -> 0 us
  between operations: 13.8 us -> 0.65 us
  local copies, waits for them, and re-layouts: 19 us -> 11.3 us
    psum x2 -> x0, waiting for transfers between devices: 349 us -> none  [the longest x1 230 us: body(): lax.psum((gain_part, bias_part), ('replica', 'outer'))]
    pallas_call x0 -> x1, Pallas kernels: none -> 168 us  [body(): pl.pallas_call(kernel, out_shape=(jax.ShapeDtypeStruct((TOK, D), BF), jax...]
    all_gather x1 -> x0, waiting for transfers between devices: 79.6 us -> none  [body(): lax.all_gather(cotangent.astype(jnp.float32), 'outer', axis=0, tiled=True)]
    all_gather x2 -> x0, blocking collectives: 78.5 us -> none  [the longest x1 59.4 us: body(): lax.all_gather(inv_std[:, 0], 'outer', axis=0, tiled=True)]
    reduce_sum x4 -> x0, other arithmetic: 17.8 us -> none  [the longest x1 7.96 us: norm_backward(): first = jnp.mean(scaled, axis=1, keepdims=True)]
    dot_general x2 -> x0, matrix products: 15.9 us -> none  [the longest x1 9.4 us: body(): lax.dot_general(hidden_cols, cot_all, (((0,), (0,)), ((), ())), preferred...]
    all_to_all x2 -> x0, starting transfers between devices: 13.1 us -> none  [the longest x1 8.45 us: body(): lax.all_to_all(tokens, 'outer', split_axis=1, concat_axis=0, tiled=True)]
    convert_element_type x2 -> x0, other arithmetic: 12.4 us -> none  [the longest x1 8.55 us: norm_backward(): return (inv_std * (scaled - first - normed * second)).astype(jnp.bfloat16)]
  transfers between devices with their start and end apart: 5 -> 0, of which waited for: 3 -> 0; matrix products, arithmetic and copies ran while one was open for 10% -> 0% of each run, Pallas kernels for 0% -> 0%
where the time goes in v1:
time: 181 us; the launch traced here: 180 us
  Pallas kernels  168 us (93%)
  local copies, waits for them, and re-layouts  11.3 us (6%)
    pallas_call x1, Pallas kernels, body(): pl.pallas_call(kernel, out_shape=(jax.ShapeDtypeStruct((TOK, D), BF), jax...  168 us
    unnamed x4, local copies, waits for them, and re-layouts  5.59 us

profile of v1, /device:TPU:1, one launch (start us, length us, event | category | flops | bytes accessed | tf_op | source)
XLA Modules:
  0.0 180.2 jit_solution(15906745271305010987)
XLA Ops:
  0.6 1.5 reshape.17.gain
  2.1 1.5 reshape.18.bias
  3.6 168.3 %shard_map.84 = (bf16[128,14848]{1,0:T(8,128)(2,1)}, bf16[928,1024]{1,0:T(8,128)(2,1)}, f32[16,16,128]{2,1,0:T(8,128)}) custom-call(bf16[128,14848]{1,0:T(8,128)(2,1)} %x.1, bf16[128,1024]{1,0:T(8,128)(2,1)} %cot.1, bf16[928,1024]{1,0:T(8,128)(2,1)} %w.1, f32[1,14848]{1,0:T(1,128)} %reshape.17.gain, f32[1,14848]{1,0:T(1,128)} %reshape.18.bias), custom_call_target="tpu_custom_call" | custom-call | tf_op jit(solution)/shard_map/pallas_call | solution.py:389
  171.9 1.0 reshape.19
  172.9 0.3 slice_reduce_fusion
  173.2 0.7 reshape_squeeze.6
  173.9 0.7 reshape_squeeze.7
  174.6 0.0 copy-start
  174.6 4.3 %copy.11 = bf16[128,14848]{1,0:T(8,128)(2,1)} copy(bf16[128,14848]{1,0:T(8,128)(2,1)} %get-tuple-element.16) | data formatting | bytes 7602176
  179.0 0.0 copy-done
  179.0 1.2 copy.12
Async XLA Ops:
  174.6 4.3 %copy-start = (bf16[928,1024]{1,0:T(8,128)(2,1)S(1)}, bf16[928,1024]{1,0:T(8,128)(2,1)}, u32[]{:S(2)}) copy-start(bf16[928,1024]{1,0:T(8,128)(2,1)} %get-tuple-element.17) | copy-start | bytes 5701636

commit v2 on v1

v2 whole, which is shorter than its diff:
```python
import jax
import jax.numpy as jnp
from jax import lax
from jax.experimental import pallas as pl
from jax.experimental.pallas import tpu as pltpu
from jax.sharding import PartitionSpec as P

BF = jnp.bfloat16
F32 = jnp.float32
MESH = pl.DeviceIdType.MESH
EPS = 1e-05

D = 14848
TOK = 128
KVW = 1024
COLS = 3712
AHEAD = 2
GH_AT = 2
N = 16
SH = D // N
BASE = (0, 256, 480, 704)
SIZE = (256, 224, 224, 224)
HBASE = (0, 128, 240, 352)
HALF = (128, 112, 112, 112)
NP = 4


def div(a, b):
    return lax.div(a, jnp.int32(b))


def rem(a, b):
    return lax.rem(a, jnp.int32(b))


def kernel(x, cot, w, gain, bias, gh_out, gw, gb, sums_out,
           xT, tok, cots, stat, stats, hid, ghs, ghT, s_buf, xr, zs, zr, fin,
           gcol, bcol, acc, gg, ggs, gtot,
           c_s, c_r, tk_s, tk_r, st_s, st_r, h_s, h_r, x_s, x_r, z_s, z_r, f_s, f_r, p_s, p_r,
           g_s, g_r, t_s, t_r, l_s):
    r = lax.axis_index("replica")
    o = lax.axis_index("outer")
    xlo, z = div(r, 8), rem(r, 8)
    xhi, y, c = div(o, 8), rem(div(o, 2), 4), rem(o, 2)

    def member(k, sign):
        dxh, dy, dc = div(k, 8), rem(div(k, 2), 4), rem(k, 2)
        xh = rem(xhi + dxh, 2)
        yy = rem(y + 4 + sign * dy, 4)
        cc = rem(c + dc, 2)
        xl = rem(xlo + dxh, 2)
        return xl * 8 + z, xh * 8 + yy * 2 + cc

    def ahead(k):
        return member(k, 1)

    def behind(k):
        return member(k, -1)

    def replica(k, sign):
        return rem(xlo + div(k, 8), 2) * 8 + rem(z + 8 + sign * rem(k, 8), 8), o

    bar = pltpu.get_barrier_semaphore()

    @pl.loop(1, N)
    def _(k):
        pl.semaphore_signal(bar, inc=1, device_id=ahead(k), device_id_type=MESH)
        pl.semaphore_signal(bar, inc=1, device_id=replica(k, 1), device_id_type=MESH)

    pl.semaphore_wait(bar, 2 * (N - 1))

    def remote(src, dst, ss, rs, dev):
        return pltpu.make_async_remote_copy(
            src_ref=src, dst_ref=dst, send_sem=ss, recv_sem=rs, device_id=dev, device_id_type=MESH)

    def rows(k, n=TOK):
        return pl.ds(pl.multiple_of(k * n, n), n)

    def cot_copy(k):
        return remote(cot, cots.at[rows(k)], c_s.at[k], c_r.at[k], ahead(k))

    def cot_forward(k):
        return remote(cots.at[rows(k)], cots.at[rows(k + 1)], c_s.at[k + 1], c_r.at[k + 1], ahead(jnp.int32(1)))

    own_cot = pltpu.make_async_copy(cot, cots.at[pl.ds(0, TOK)], l_s.at[0])
    own_cot.start()
    cot_copy(jnp.int32(1)).start()

    @pl.loop(1, 8)
    def _(j):
        cot_copy(2 * j).start()

    def turn(t, total):
        s = pl.multiple_of(t * 512, 512)
        v = x[:, pl.ds(s, 512)].T
        xT[pl.ds(s, 512), :] = v
        return total + v.astype(F32).reshape(64, 8, TOK).sum(0)

    total = lax.fori_loop(0, D // 512, turn, jnp.zeros((8, TOK), F32))
    mean = total.sum(0, keepdims=True) / D

    def tok_copy(k, part):
        dev = ahead(k)
        at = pl.multiple_of(dev[1] * SH + BASE[part], 16)
        return remote(xT.at[pl.ds(at, SIZE[part])], tok.at[k, pl.ds(BASE[part], SIZE[part])],
                      tk_s.at[part, k], tk_r.at[part, k], dev)

    own_tok = pltpu.make_async_copy(xT.at[rows(o, SH)], tok.at[0], l_s.at[1])
    own_tok.start()
    def tok_start(part):
        @pl.loop(1, N)
        def _(k):
            tok_copy(k, part).start()

    for part in range(AHEAD):
        tok_start(part)

    def spread(t, total):
        s = pl.multiple_of(t * 512, 512)
        v = xT[pl.ds(s, 512), :].astype(F32) - mean
        return total + (v * v).reshape(64, 8, TOK).sum(0)

    total = lax.fori_loop(0, D // 512, spread, jnp.zeros((8, TOK), F32))
    inv = lax.rsqrt(total.sum(0, keepdims=True) / D + EPS)
    stat[0:1, :] = mean
    stat[1:2, :] = inv
    stats[0, 0:1, :] = mean
    stats[0, 1:2, :] = inv

    def stat_copy(k):
        return remote(stat, stats.at[k], st_s.at[k], st_r.at[k], ahead(k))

    @pl.loop(1, N)
    def _(k):
        stat_copy(k).start()

    first_tile = div(o * SH, 128)
    shift = pl.multiple_of(rem(o, 4) * 32, 32)
    for t in range(8):
        gcol[t * 128:t * 128 + 128, :] = jnp.broadcast_to(gain[pl.ds(first_tile + t, 1), :], (TOK, 128)).T
        bcol[t * 128:t * 128 + 128, :] = jnp.broadcast_to(bias[pl.ds(first_tile + t, 1), :], (TOK, 128)).T

    @pl.loop(1, 8)
    def _(j):
        cot_copy(2 * j).wait_recv()
        cot_forward(2 * j).start()

    own_cot.wait()

    @pl.loop(0, 8)
    def _(j):
        @pl.when(j == 0)
        def _():
            cot_copy(jnp.int32(1)).wait_recv()

        @pl.when(j > 0)
        def _():
            cot_forward(2 * j).wait_recv()

        v = lax.dot_general(w[...], cots[rows(j, 2 * TOK), :], (((1,), (1,)), ((), ())),
                            preferred_element_type=F32).astype(BF)
        ghs[2 * j] = v[:, :TOK]
        ghs[2 * j + 1] = v[:, TOK:]

    own_tok.wait()
    acc[...] = jnp.zeros_like(acc)

    def gh_copy(k):
        return remote(ghs.at[k], ghT.at[rows(o, SH)], h_s.at[k], h_r.at[k], behind(k))

    own_gh = pltpu.make_async_copy(ghs.at[0], ghT.at[rows(o, SH)], l_s.at[2])
    own_gh.start()

    beside = replica(jnp.int32(8), 1)

    def half_copy(part):
        h = HALF[part]
        at = pl.multiple_of(BASE[part] + (1 - xlo) * h, 16)
        return remote(s_buf.at[:, pl.ds(at, h)], xr.at[:, pl.ds(HBASE[part], h)], x_s.at[part], x_r.at[part], beside)

    def z_copy(part, k):
        at = pl.ds(HBASE[part], HALF[part])
        return remote(zs.at[rem(z + k, 8), at], zr.at[k, at], z_s.at[part, k], z_r.at[part, k], replica(k, 1))

    def gw_at(part, zz):
        return gw.at[pl.ds(pl.multiple_of(BASE[part] + xlo * HALF[part], 16), HALF[part]), rows(zz)]

    def fin_copy(part, k):
        return remote(fin.at[pl.ds(HBASE[part], HALF[part])], gw_at(part, z), f_s.at[part, k], f_r.at[part, k],
                      replica(k, 1))

    def pass_copy(part, k):
        here = gw_at(part, rem(z + 8 - k, 8))
        return remote(here, here, p_s.at[part, k], p_r.at[part, k], beside)

    def weight_part(part):
        base, size = BASE[part], SIZE[part]

        @pl.loop(1, N)
        def _(k):
            tok_copy(k, part).wait_recv()
            if part == 0:
                stat_copy(k).wait_recv()

        if part + AHEAD < NP:
            tok_start(part + AHEAD)

        step = size // 2
        for u in range(2):
            lo = base + u * step

            def block(k, carry):
                ag, ab = carry
                normed = (tok[k, lo:lo + step, :].astype(F32) - stats[k, 0:1, :]) * stats[k, 1:2, :]
                at = pl.multiple_of(shift + lo, 16)
                hid[u * step:(u + 1) * step, rows(k)] = (
                    gcol[pl.ds(at, step), :] * normed + bcol[pl.ds(at, step), :]).astype(BF)
                gh = ghs[k, lo:lo + step, :].astype(F32)
                return ag + gh * normed, ab + gh

            zero = jnp.zeros((step, TOK), F32)
            ag, ab = lax.fori_loop(0, N, block, (zero, zero))
            at = pl.multiple_of(shift + lo, 16)
            acc[0, pl.ds(at, step), :] = ag
            acc[1, pl.ds(at, step), :] = ab

        @pl.loop(0, 4)
        def _(n):
            v = jnp.dot(hid[0:size, :], cots[:, rows(n, 256)], preferred_element_type=F32).astype(BF)
            s_buf[2 * n, base:base + size, :] = v[:, :128]
            s_buf[2 * n + 1, base:base + size, :] = v[:, 128:]

        half_copy(part).start()

    def beside_part(part):
        h, hb = HALF[part], HBASE[part]
        half_copy(part).wait_recv()
        at = pl.multiple_of(BASE[part] + xlo * h, 16)
        for n in range(8):
            zs[n, hb:hb + h, :] = (
                s_buf[n, pl.ds(at, h), :].astype(F32) + xr[n, hb:hb + h, :].astype(F32)).astype(BF)

        @pl.loop(1, 8)
        def _(k):
            z_copy(part, k).start()

    def own_part(part):
        h, hb = HALF[part], HBASE[part]

        @pl.loop(1, 8)
        def _(k):
            z_copy(part, k).wait_recv()

        at = pl.multiple_of(BASE[part] + xlo * h, 16)
        v = s_buf[z, pl.ds(at, h), :].astype(F32) + xr[z, hb:hb + h, :].astype(F32)
        for k in range(1, 8):
            v = v + zr[k, hb:hb + h, :].astype(F32)
        v = (v / N).astype(BF)
        fin[hb:hb + h, :] = v
        gw[pl.ds(at, h), rows(z)] = v

        @pl.loop(1, 8)
        def _(k):
            fin_copy(part, k).start()

        pass_copy(part, jnp.int32(0)).start()

    def pass_part(part):
        @pl.loop(1, 8)
        def _(k):
            fin_copy(part, k).wait_recv()
            pass_copy(part, k).start()

    def gg_copy(k):
        return remote(gg, ggs.at[r], g_s.at[k], g_r.at[k], replica(k, 1))

    def gt_copy(k):
        return remote(gtot, gb.at[o], t_s.at[k], t_r.at[k], ahead(k))

    for i in range(NP + 3):
        if i < NP:
            weight_part(i)
        if i == GH_AT:
            @pl.loop(1, N)
            def _(k):
                gh_copy(k).start()
        if i == NP - 1:
            for j in (0, 1):
                for t in range(8):
                    gg[j * 8 + t:j * 8 + t + 1, :] = acc[j, t * 128:t * 128 + 128, :].T.sum(0, keepdims=True)
            ggs[r] = gg[...]

            @pl.loop(1, N)
            def _(k):
                gg_copy(k).start()
        if 0 <= i - 1 < NP:
            beside_part(i - 1)
        if 0 <= i - 2 < NP:
            own_part(i - 2)
        if 0 <= i - 3 < NP:
            pass_part(i - 3)
        if i == NP:
            @pl.loop(1, N)
            def _(k):
                gg_copy(k).wait_recv()

            gtot[...] = ggs[...].sum(0) / N
            gb[o] = gtot[...]

            @pl.loop(1, N)
            def _(k):
                gt_copy(k).start()

    stat_t = jnp.broadcast_to(stat[0:1, :], (TOK, TOK)).T
    inv_t = jnp.broadcast_to(stat[1:2, :], (TOK, TOK)).T
    own_gh.wait()

    def piece(s, n, sums):
        g = ghT[pl.ds(s, n), :].T
        gh_out[:, pl.ds(s, n)] = g
        a, b = sums
        for t in range(n // 128):
            at = pl.multiple_of(s + t * 128, 128)
            scaled = g[:, t * 128:t * 128 + 128].astype(F32) * gain[pl.ds(div(s, 128) + t, 1), :]
            normed = (x[:, pl.ds(at, 128)].astype(F32) - stat_t) * inv_t
            a = a + scaled
            b = b + scaled * normed
        return a, b

    quarter = 2 * xhi + div(y, 2)
    sums = (jnp.zeros((TOK, TOK), F32), jnp.zeros((TOK, TOK), F32))

    def quarter_step(q, sums):
        qq = rem(quarter + q, 4)
        for m in range(4):
            po = qq * 4 + m
            pxh, py, pc = div(po, 8), rem(div(po, 2), 4), rem(po, 2)
            k = rem(pxh + xhi, 2) * 8 + rem(py + 4 - y, 4) * 2 + rem(pc + c, 2)

            @pl.when(k > 0)
            def _():
                gh_copy(k).wait_recv()

        start = qq * 3712

        def inner(t, sums):
            return piece(pl.multiple_of(start + t * 512, 128), 512, sums)

        sums = lax.fori_loop(0, 7, inner, sums)
        return piece(pl.multiple_of(start + 3584, 128), 128, sums)

    sums = lax.fori_loop(0, 4, quarter_step, sums)
    sums_out[0] = stat_t
    sums_out[1] = inv_t
    sums_out[2] = jnp.broadcast_to(sums[0].sum(1, keepdims=True) / D, (TOK, TOK))
    sums_out[3] = jnp.broadcast_to(sums[1].sum(1, keepdims=True) / D, (TOK, TOK))

    for part in range(NP):
        pass_copy(part, jnp.int32(0)).wait_recv()
        pass_copy(part, jnp.int32(0)).wait_send()
        half_copy(part).wait_send()

        @pl.loop(1, 8)
        def _(k):
            pass_copy(part, k).wait_recv()
            pass_copy(part, k).wait_send()
            fin_copy(part, k).wait_send()
            z_copy(part, k).wait_send()

        @pl.loop(1, N)
        def _(k):
            tok_copy(k, part).wait_send()

    @pl.loop(1, N)
    def _(k):
        gt_copy(k).wait_recv()
        stat_copy(k).wait_send()
        gh_copy(k).wait_send()
        gg_copy(k).wait_send()
        gt_copy(k).wait_send()

    cot_copy(jnp.int32(1)).wait_send()

    @pl.loop(1, 8)
    def _(j):
        cot_copy(2 * j).wait_send()
        cot_forward(2 * j).wait_send()


def finish(x, gh, gain, sums, gw, gb, out, gw_out, gg_out):
    t = pl.program_id(0)

    @pl.when(t == 0)
    def _():
        gw_out[...] = gw[...]
        gg_out[...] = jnp.zeros_like(gg_out)
        for j in (0, 1):
            for m in range(N):
                at = 29 * (m // 4) + 7 * (m % 4)
                gg_out[j, at:at + 8, :] += gb[m, 8 * j:8 * j + 8, :]

    for u in range(COLS // 128):
        at = slice(u * 128, u * 128 + 128)
        scaled = gh[:, at].astype(F32) * gain[pl.ds(t * (COLS // 128) + u, 1), :]
        normed = (x[:, at].astype(F32) - sums[0]) * sums[1]
        out[:, at] = (sums[1] * (scaled - sums[2] - normed * sums[3])).astype(BF)


def body(tokens, cotangent, kv_weight, gain, bias):
    V = pl.BlockSpec(memory_space=pltpu.VMEM)
    half = SH // 2
    scratch = [
        pltpu.VMEM((D, TOK), BF),
        pltpu.VMEM((N, SH, TOK), BF),
        pltpu.VMEM((N * TOK, KVW), BF),
        pltpu.VMEM((8, TOK), F32),
        pltpu.VMEM((N, 8, TOK), F32),
        pltpu.VMEM((max(SIZE), N * TOK), BF),
        pltpu.VMEM((N, SH, TOK), BF),
        pltpu.VMEM((D, TOK), BF),
        pltpu.VMEM((8, SH, 128), BF),
        pltpu.VMEM((8, half, 128), BF),
        pltpu.VMEM((8, half, 128), BF),
        pltpu.VMEM((8, half, 128), BF),
        pltpu.VMEM((half, 128), BF),
        pltpu.VMEM((1024, TOK), F32),
        pltpu.VMEM((1024, TOK), F32),
        pltpu.VMEM((2, 1024, TOK), F32),
        pltpu.VMEM((N, 128), F32),
        pltpu.VMEM((N, N, 128), F32),
        pltpu.VMEM((N, 128), F32),
    ]
    dma = pltpu.SemaphoreType.DMA
    sems = ([dma((N,))] * 2 + [dma((NP, N))] * 2 + [dma((N,))] * 4 + [dma((NP,))] * 2
            + [dma((NP, 8))] * 6 + [dma((N,))] * 4 + [dma((3,))])
    gain, bias = gain.reshape(D // 128, 128), bias.reshape(D // 128, 128)
    gh, gw, gb, sums = pl.pallas_call(
        kernel,
        out_shape=(
            jax.ShapeDtypeStruct((TOK, D), BF),
            jax.ShapeDtypeStruct((SH, KVW), BF),
            jax.ShapeDtypeStruct((N, N, 128), F32),
            jax.ShapeDtypeStruct((4, TOK, TOK), F32),
        ),
        in_specs=[V] * 5,
        out_specs=(V, V, V, V),
        scratch_shapes=scratch + sems,
        compiler_params=pltpu.CompilerParams(
            collective_id=0, has_side_effects=True, vmem_limit_bytes=60 << 20),
    )(tokens, cotangent, kv_weight, gain, bias)
    tile = pl.BlockSpec((TOK, COLS), lambda t: (0, t))
    out, gw, gg = pl.pallas_call(
        finish,
        grid=(D // COLS,),
        out_shape=(
            jax.ShapeDtypeStruct((TOK, D), BF),
            jax.ShapeDtypeStruct((SH, KVW), BF),
            jax.ShapeDtypeStruct((2, D // 128, 128), F32),
        ),
        in_specs=[tile, tile, V, V, V, V],
        out_specs=(tile, V, V),
        compiler_params=pltpu.CompilerParams(vmem_limit_bytes=60 << 20),
    )(tokens, gh, gain, sums, gw, gb)
    return out, gw, gg[0].reshape(D), gg[1].reshape(D)


def solution(mesh):
    in_specs = (
        P(("replica", "outer"), None),
        P(("replica", "outer"), None),
        P("outer", None),
        P(),
        P(),
    )
    out_specs = (P(("replica", "outer"), None), P("outer", None), P(), P())
    return jax.shard_map(body, mesh=mesh, in_specs=in_specs, out_specs=out_specs, check_vma=False)
```

time: 181 us -> 146 us (0.81)
  Pallas kernels: 168 us -> 143 us
  local copies, waits for them, and re-layouts: 11.3 us -> 1.51 us
    pallas_call x1, Pallas kernels: 168 us -> 135 us  [body(): pl.pallas_call(kernel, out_shape=(jax.ShapeDtypeStruct((TOK, D), BF), jax...]
    pallas_call x0 -> x1, Pallas kernels: none -> 7.74 us  [body(): pl.pallas_call(finish, grid=(D // COLS,), out_shape=(jax.ShapeDtypeStruct...]
    unnamed x4 -> x0, local copies, waits for them, and re-layouts: 5.59 us -> none
    reshape x3 -> x0, local copies, waits for them, and re-layouts: 3.96 us -> none  [the longest x1 1.49 us: body(): gain.reshape(1, D)]
where the time goes in v2:
time: 146 us; the launch traced here: 145 us
  Pallas kernels  143 us (98%)
  local copies, waits for them, and re-layouts  1.51 us (1%)
    pallas_call x1, Pallas kernels, body(): pl.pallas_call(kernel, out_shape=(jax.ShapeDtypeStruct((TOK, D), BF), jax...  135 us
    pallas_call x1, Pallas kernels, body(): pl.pallas_call(finish, grid=(D // COLS,), out_shape=(jax.ShapeDtypeStruct...  7.74 us

profile of v2, /device:TPU:1, one launch (start us, length us, event | category | flops | bytes accessed | tf_op | source)
XLA Modules:
  0.0 144.9 jit_solution(9433551825443667114)
XLA Ops:
  0.6 135.0 %shard_map.84 = (bf16[128,14848]{1,0:T(8,128)(2,1)}, bf16[928,1024]{1,0:T(8,128)(2,1)}, f32[16,16,128]{2,1,0:T(8,128)}, f32[4,128,128]{2,1,0:T(8,128)}) custom-call(bf16[128,14848]{1,0:T(8,128)(2,1)} %x.3, bf16[128,1024]{1,0:T(8,128)(2,1)} %cot.1, bf16[928,1024]{1,0:T(8,128)(2,1)} %w.1, f32[116,128]{1,0:T(8,128)} %bitcast.6, f32[116,128]{1,0:T(8,128)} %bitcast.8), custom_call_target="tpu_custom_call" | custom-call | tf_op jit(solution)/shard_map/pallas_call | solution.py:437
  135.7 7.7 %shard_map.85 = (bf16[128,14848]{1,0:T(8,128)(2,1)}, bf16[928,1024]{1,0:T(8,128)(2,1)}, f32[2,116,128]{2,1,0:T(8,128)}) custom-call(bf16[128,14848]{1,0:T(8,128)(2,1)} %x.3, bf16[128,14848]{1,0:T(8,128)(2,1)} %get-tuple-element.11.gh, f32[116,128]{1,0:T(8,128)} %bitcast.7, f32[4,128,128]{2,1,0:T(8,128)} %get-tuple-element.12.sums, ...), custom_call_target="tpu_custom_call" | custom-call | tf_op jit(solution)/shard_map/pallas_call | solution.py:452
  143.4 1.5 %slice_bitcast_fusion = (f32[14848]{0:T(1024)}, f32[14848]{0:T(1024)}) fusion(f32[2,116,128]{2,1,0:T(8,128)} %get-tuple-element.17), kind=kLoop, calls=%fused_computation | loop fusion | bytes 237568 | tf_op jit(solution)/shard_map/reshape;squeeze | solution.py:464

commit v3 on v2

--- a/solution.py
+++ b/solution.py
@@ -15,14 +15,14 @@
 KVW = 1024
 COLS = 3712
 AHEAD = 2
-GH_AT = 2
+GH_AT = 3
 N = 16
 SH = D // N
-BASE = (0, 256, 480, 704)
-SIZE = (256, 224, 224, 224)
-HBASE = (0, 128, 240, 352)
-HALF = (128, 112, 112, 112)
-NP = 4
+BASE = (0, 192, 384, 576, 768)
+SIZE = (192, 192, 192, 192, 160)
+HBASE = (0, 96, 192, 288, 384)
+HALF = (96, 96, 96, 96, 80)
+NP = 5
 
 
 def div(a, b):
@@ -33,11 +33,11 @@
     return lax.rem(a, jnp.int32(b))
 
 
-def kernel(x, cot, w, gain, bias, gh_out, gw, gb, sums_out,
-           xT, tok, cots, stat, stats, hid, ghs, ghT, s_buf, xr, zs, zr, fin,
-           gcol, bcol, acc, gg, ggs, gtot,
-           c_s, c_r, tk_s, tk_r, st_s, st_r, h_s, h_r, x_s, x_r, z_s, z_r, f_s, f_r, p_s, p_r,
-           g_s, g_r, t_s, t_r, l_s):
+def kernel(x_hbm, cot, w_hbm, gain, bias, ghT, gw, gb, sums_out,
+           x, w, xT, tok, cots, stat, stats, hid, ghs, s_buf, xr, zs, zr, fin,
+           gcol, bcol, acc, gg, ggs, gtot, tsum, tsums,
+           c_s, c_r, e_s, e_r, tk_s, tk_r, st_s, st_r, h_s, h_r, x_s, x_r, z_s, z_r, f_s, f_r, p_s, p_r,
+           g_s, g_r, t_s, t_r, u_s, u_r, l_s):
     r = lax.axis_index("replica")
     o = lax.axis_index("outer")
     xlo, z = div(r, 8), rem(r, 8)
@@ -67,8 +67,6 @@
         pl.semaphore_signal(bar, inc=1, device_id=ahead(k), device_id_type=MESH)
         pl.semaphore_signal(bar, inc=1, device_id=replica(k, 1), device_id_type=MESH)
 
-    pl.semaphore_wait(bar, 2 * (N - 1))
-
     def remote(src, dst, ss, rs, dev):
         return pltpu.make_async_remote_copy(
             src_ref=src, dst_ref=dst, send_sem=ss, recv_sem=rs, device_id=dev, device_id_type=MESH)
@@ -76,19 +74,32 @@
     def rows(k, n=TOK):
         return pl.ds(pl.multiple_of(k * n, n), n)
 
+    x_in = pltpu.make_async_copy(x_hbm, x, l_s.at[3])
+    x_in.start()
+    w_in = pltpu.make_async_copy(w_hbm, w, l_s.at[4])
+    w_in.start()
+
     def cot_copy(k):
         return remote(cot, cots.at[rows(k)], c_s.at[k], c_r.at[k], ahead(k))
 
+    def cot_along_y(j):
+        at = pl.multiple_of((8 + 2 * j) * TOK, TOK)
+        return remote(cots.at[pl.ds(8 * TOK, TOK // 2)], cots.at[pl.ds(at, TOK // 2)],
+                      c_s.at[8 + 2 * j], c_r.at[8 + 2 * j], ahead(2 * j))
+
+    def cot_along_x(j):
+        at = pl.multiple_of((8 + 2 * j) * TOK + TOK // 2, TOK // 2)
+        here = pl.multiple_of(2 * j * TOK + TOK // 2, TOK // 2)
+        return remote(cots.at[pl.ds(here, TOK // 2)], cots.at[pl.ds(at, TOK // 2)],
+                      e_s.at[j], e_r.at[j], ahead(jnp.int32(8)))
+
     def cot_forward(k):
         return remote(cots.at[rows(k)], cots.at[rows(k + 1)], c_s.at[k + 1], c_r.at[k + 1], ahead(jnp.int32(1)))
 
     own_cot = pltpu.make_async_copy(cot, cots.at[pl.ds(0, TOK)], l_s.at[0])
     own_cot.start()
-    cot_copy(jnp.int32(1)).start()
-
-    @pl.loop(1, 8)
-    def _(j):
-        cot_copy(2 * j).start()
+
+    x_in.wait()
 
     def turn(t, total):
         s = pl.multiple_of(t * 512, 512)
@@ -98,6 +109,14 @@
 
     total = lax.fori_loop(0, D // 512, turn, jnp.zeros((8, TOK), F32))
     mean = total.sum(0, keepdims=True) / D
+
+    pl.semaphore_wait(bar, 2 * (N - 1))
+    cot_copy(jnp.int32(8)).start()
+    cot_copy(jnp.int32(1)).start()
+
+    @pl.loop(1, 4)
+    def _(j):
+        cot_copy(2 * j).start()
 
     def tok_copy(k, part):
         dev = ahead(k)
@@ -140,36 +159,35 @@
         gcol[t * 128:t * 128 + 128, :] = jnp.broadcast_to(gain[pl.ds(first_tile + t, 1), :], (TOK, 128)).T
         bcol[t * 128:t * 128 + 128, :] = jnp.broadcast_to(bias[pl.ds(first_tile + t, 1), :], (TOK, 128)).T
 
-    @pl.loop(1, 8)
+    cot_copy(jnp.int32(8)).wait_recv()
+
+    @pl.loop(1, 4)
+    def _(j):
+        cot_along_y(j).start()
+
+    cot_forward(jnp.int32(8)).start()
+
+    @pl.loop(1, 4)
     def _(j):
         cot_copy(2 * j).wait_recv()
+        cot_along_x(j).start()
         cot_forward(2 * j).start()
 
+    @pl.loop(1, 4)
+    def _(j):
+        cot_along_y(j).wait_recv()
+        cot_along_x(j).wait_recv()
+        cot_forward(8 + 2 * j).start()
+
     own_cot.wait()
-
-    @pl.loop(0, 8)
-    def _(j):
-        @pl.when(j == 0)
-        def _():
-            cot_copy(jnp.int32(1)).wait_recv()
-
-        @pl.when(j > 0)
-        def _():
-            cot_forward(2 * j).wait_recv()
-
-        v = lax.dot_general(w[...], cots[rows(j, 2 * TOK), :], (((1,), (1,)), ((), ())),
-                            preferred_element_type=F32).astype(BF)
-        ghs[2 * j] = v[:, :TOK]
-        ghs[2 * j + 1] = v[:, TOK:]
+    w_in.wait()
+    tsum[...] = jnp.zeros_like(tsum)
 
     own_tok.wait()
     acc[...] = jnp.zeros_like(acc)
 
     def gh_copy(k):
         return remote(ghs.at[k], ghT.at[rows(o, SH)], h_s.at[k], h_r.at[k], behind(k))
-
-    own_gh = pltpu.make_async_copy(ghs.at[0], ghT.at[rows(o, SH)], l_s.at[2])
-    own_gh.start()
 
     beside = replica(jnp.int32(8), 1)
 
@@ -193,17 +211,19 @@
         here = gw_at(part, rem(z + 8 - k, 8))
         return remote(here, here, p_s.at[part, k], p_r.at[part, k], beside)
 
-    def weight_part(part):
-        base, size = BASE[part], SIZE[part]
-
+    def receive_part(part):
         @pl.loop(1, N)
         def _(k):
             tok_copy(k, part).wait_recv()
             if part == 0:
                 stat_copy(k).wait_recv()
-
-        if part + AHEAD < NP:
-            tok_start(part + AHEAD)
+            if part + AHEAD < NP:
+                tok_copy(k, part + AHEAD).start()
+            if part == GH_AT:
+                gh_copy(k).start()
+
+    def weight_part(part):
+        base, size = BASE[part], SIZE[part]
 
         step = size // 2
         for u in range(2):
@@ -216,6 +236,9 @@
                 hid[u * step:(u + 1) * step, rows(k)] = (
                     gcol[pl.ds(at, step), :] * normed + bcol[pl.ds(at, step), :]).astype(BF)
                 gh = ghs[k, lo:lo + step, :].astype(F32)
+                scaled = gcol[pl.ds(at, step), :] * gh
+                tsum[k, 0:8, :] += scaled.reshape(step // 8, 8, TOK).sum(0)
+                tsum[k, 8:16, :] += (scaled * normed).reshape(step // 8, 8, TOK).sum(0)
                 return ag + gh * normed, ab + gh
 
             zero = jnp.zeros((step, TOK), F32)
@@ -274,16 +297,37 @@
     def gg_copy(k):
         return remote(gg, ggs.at[r], g_s.at[k], g_r.at[k], replica(k, 1))
 
+    def sum_copy(k):
+        return remote(tsum.at[k], tsums.at[k], u_s.at[k], u_r.at[k], behind(k))
+
     def gt_copy(k):
         return remote(gtot, gb.at[o], t_s.at[k], t_r.at[k], ahead(k))
 
+    receive_part(0)
+
+    @pl.loop(0, 8)
+    def _(j):
+        @pl.when(j == 0)
+        def _():
+            cot_copy(jnp.int32(1)).wait_recv()
+
+        @pl.when(j > 0)
+        def _():
+            cot_forward(2 * j).wait_recv()
+
+        v = lax.dot_general(w[...], cots[rows(j, 2 * TOK), :], (((1,), (1,)), ((), ())),
+                            preferred_element_type=F32).astype(BF)
+        ghs[2 * j] = v[:, :TOK]
+        ghs[2 * j + 1] = v[:, TOK:]
+
+    own_gh = pltpu.make_async_copy(ghs.at[0], ghT.at[rows(o, SH)], l_s.at[2])
+    own_gh.start()
+
     for i in range(NP + 3):
         if i < NP:
+            if i > 0:
+                receive_part(i)
             weight_part(i)
-        if i == GH_AT:
-            @pl.loop(1, N)
-            def _(k):
-                gh_copy(k).start()
         if i == NP - 1:
             for j in (0, 1):
                 for t in range(8):
@@ -292,6 +336,7 @@
 
             @pl.loop(1, N)
             def _(k):
+                sum_copy(k).start()
                 gg_copy(k).start()
         if 0 <= i - 1 < NP:
             beside_part(i - 1)
@@ -311,49 +356,19 @@
             def _(k):
                 gt_copy(k).start()
 
-    stat_t = jnp.broadcast_to(stat[0:1, :], (TOK, TOK)).T
-    inv_t = jnp.broadcast_to(stat[1:2, :], (TOK, TOK)).T
+    total = tsum[0]
+    for k in range(1, N):
+        sum_copy(jnp.int32(k)).wait_recv()
+        total = total + tsums[k]
+    sums_out[0:2, :] = stat[0:2, :]
+    sums_out[2:3, :] = total[0:8].sum(0, keepdims=True) / D
+    sums_out[3:4, :] = total[8:16].sum(0, keepdims=True) / D
+    sums_out[4:8, :] = jnp.zeros((4, TOK), F32)
     own_gh.wait()
 
-    def piece(s, n, sums):
-        g = ghT[pl.ds(s, n), :].T
-        gh_out[:, pl.ds(s, n)] = g
-        a, b = sums
-        for t in range(n // 128):
-            at = pl.multiple_of(s + t * 128, 128)
-            scaled = g[:, t * 128:t * 128 + 128].astype(F32) * gain[pl.ds(div(s, 128) + t, 1), :]
-            normed = (x[:, pl.ds(at, 128)].astype(F32) - stat_t) * inv_t
-            a = a + scaled
-            b = b + scaled * normed
-        return a, b
-
-    quarter = 2 * xhi + div(y, 2)
-    sums = (jnp.zeros((TOK, TOK), F32), jnp.zeros((TOK, TOK), F32))
-
-    def quarter_step(q, sums):
-        qq = rem(quarter + q, 4)
-        for m in range(4):
-            po = qq * 4 + m
-            pxh, py, pc = div(po, 8), rem(div(po, 2), 4), rem(po, 2)
-            k = rem(pxh + xhi, 2) * 8 + rem(py + 4 - y, 4) * 2 + rem(pc + c, 2)
-
-            @pl.when(k > 0)
-            def _():
-                gh_copy(k).wait_recv()
-
-        start = qq * 3712
-
-        def inner(t, sums):
-            return piece(pl.multiple_of(start + t * 512, 128), 512, sums)
-
-        sums = lax.fori_loop(0, 7, inner, sums)
-        return piece(pl.multiple_of(start + 3584, 128), 128, sums)
-
-    sums = lax.fori_loop(0, 4, quarter_step, sums)
-    sums_out[0] = stat_t
-    sums_out[1] = inv_t
-    sums_out[2] = jnp.broadcast_to(sums[0].sum(1, keepdims=True) / D, (TOK, TOK))
-    sums_out[3] = jnp.broadcast_to(sums[1].sum(1, keepdims=True) / D, (TOK, TOK))
+    @pl.loop(1, N)
+    def _(k):
+        gh_copy(k).wait_recv()
 
     for part in range(NP):
         pass_copy(part, jnp.int32(0)).wait_recv()
@@ -374,42 +389,61 @@
     @pl.loop(1, N)
     def _(k):
         gt_copy(k).wait_recv()
+        sum_copy(k).wait_send()
         stat_copy(k).wait_send()
         gh_copy(k).wait_send()
         gg_copy(k).wait_send()
         gt_copy(k).wait_send()
 
     cot_copy(jnp.int32(1)).wait_send()
-
-    @pl.loop(1, 8)
+    cot_copy(jnp.int32(8)).wait_send()
+    cot_forward(jnp.int32(8)).wait_send()
+
+    @pl.loop(1, 4)
     def _(j):
         cot_copy(2 * j).wait_send()
+        cot_along_x(j).wait_send()
+        cot_along_y(j).wait_send()
         cot_forward(2 * j).wait_send()
-
-
-def finish(x, gh, gain, sums, gw, gb, out, gw_out, gg_out):
+        cot_forward(8 + 2 * j).wait_send()
+
+
+def finish(x, ghT, gain, sums, gw, gb, out, gw_out, gain_out, bias_out, col):
     t = pl.program_id(0)
 
     @pl.when(t == 0)
     def _():
-        gw_out[...] = gw[...]
-        gg_out[...] = jnp.zeros_like(gg_out)
-        for j in (0, 1):
+        for j, total in enumerate((gain_out, bias_out)):
+            total[...] = jnp.zeros_like(total)
             for m in range(N):
                 at = 29 * (m // 4) + 7 * (m % 4)
-                gg_out[j, at:at + 8, :] += gb[m, 8 * j:8 * j + 8, :]
-
-    for u in range(COLS // 128):
-        at = slice(u * 128, u * 128 + 128)
-        scaled = gh[:, at].astype(F32) * gain[pl.ds(t * (COLS // 128) + u, 1), :]
-        normed = (x[:, at].astype(F32) - sums[0]) * sums[1]
-        out[:, at] = (sums[1] * (scaled - sums[2] - normed * sums[3])).astype(BF)
+                total[at:at + 8, :] += gb[m, 8 * j:8 * j + 8, :]
+        for j in range(4):
+            col[j] = jnp.broadcast_to(sums[j:j + 1, :], (TOK, TOK)).T
+
+    gw_out[...] = gw[...]
+
+    def piece(at, n):
+        g = ghT[pl.ds(at, n), :].T
+        for u in range(n // 128):
+            tile = pl.ds(at + u * 128, 128)
+            scaled = g[:, u * 128:u * 128 + 128].astype(F32) * gain[pl.ds(t * (COLS // 128) + at // 128 + u, 1), :]
+            normed = (x[:, tile].astype(F32) - col[0]) * col[1]
+            out[:, tile] = (col[1] * (scaled - col[2] - normed * col[3])).astype(BF)
+
+    @pl.loop(0, COLS // 512)
+    def _(i):
+        piece(pl.multiple_of(i * 512, 512), 512)
+
+    piece(COLS // 512 * 512, COLS % 512)
 
 
 def body(tokens, cotangent, kv_weight, gain, bias):
     V = pl.BlockSpec(memory_space=pltpu.VMEM)
     half = SH // 2
     scratch = [
+        pltpu.VMEM((TOK, D), BF),
+        pltpu.VMEM((SH, KVW), BF),
         pltpu.VMEM((D, TOK), BF),
         pltpu.VMEM((N, SH, TOK), BF),
         pltpu.VMEM((N * TOK, KVW), BF),
@@ -417,7 +451,6 @@
         pltpu.VMEM((N, 8, TOK), F32),
         pltpu.VMEM((max(SIZE), N * TOK), BF),
         pltpu.VMEM((N, SH, TOK), BF),
-        pltpu.VMEM((D, TOK), BF),
         pltpu.VMEM((8, SH, 128), BF),
         pltpu.VMEM((8, half, 128), BF),
         pltpu.VMEM((8, half, 128), BF),
@@ -429,39 +462,46 @@
         pltpu.VMEM((N, 128), F32),
         pltpu.VMEM((N, N, 128), F32),
         pltpu.VMEM((N, 128), F32),
+        pltpu.VMEM((N, N, TOK), F32),
+        pltpu.VMEM((N, N, TOK), F32),
     ]
     dma = pltpu.SemaphoreType.DMA
-    sems = ([dma((N,))] * 2 + [dma((NP, N))] * 2 + [dma((N,))] * 4 + [dma((NP,))] * 2
-            + [dma((NP, 8))] * 6 + [dma((N,))] * 4 + [dma((3,))])
+    sems = ([dma((N,))] * 2 + [dma((4,))] * 2 + [dma((NP, N))] * 2 + [dma((N,))] * 4 + [dma((NP,))] * 2
+            + [dma((NP, 8))] * 6 + [dma((N,))] * 6 + [dma((5,))])
     gain, bias = gain.reshape(D // 128, 128), bias.reshape(D // 128, 128)
-    gh, gw, gb, sums = pl.pallas_call(
+    A = pl.BlockSpec(memory_space=pl.ANY)
+    ghT, gw, gb, sums = pl.pallas_call(
         kernel,
         out_shape=(
-            jax.ShapeDtypeStruct((TOK, D), BF),
+            jax.ShapeDtypeStruct((D, TOK), BF),
             jax.ShapeDtypeStruct((SH, KVW), BF),
             jax.ShapeDtypeStruct((N, N, 128), F32),
-            jax.ShapeDtypeStruct((4, TOK, TOK), F32),
+            jax.ShapeDtypeStruct((8, TOK), F32),
         ),
-        in_specs=[V] * 5,
-        out_specs=(V, V, V, V),
+        in_specs=[A, V, A, V, V],
+        out_specs=(A, V, V, V),
         scratch_shapes=scratch + sems,
         compiler_params=pltpu.CompilerParams(
             collective_id=0, has_side_effects=True, vmem_limit_bytes=60 << 20),
     )(tokens, cotangent, kv_weight, gain, bias)
     tile = pl.BlockSpec((TOK, COLS), lambda t: (0, t))
-    out, gw, gg = pl.pallas_call(
+    turned = pl.BlockSpec((COLS, TOK), lambda t: (t, 0))
+    weight = pl.BlockSpec((SH, KVW * COLS // D), lambda t: (0, t))
+    out, gw, gain_sum, bias_sum = pl.pallas_call(
         finish,
         grid=(D // COLS,),
         out_shape=(
             jax.ShapeDtypeStruct((TOK, D), BF),
             jax.ShapeDtypeStruct((SH, KVW), BF),
-            jax.ShapeDtypeStruct((2, D // 128, 128), F32),
+            jax.ShapeDtypeStruct((D // 128, 128), F32),
+            jax.ShapeDtypeStruct((D // 128, 128), F32),
         ),
-        in_specs=[tile, tile, V, V, V, V],
-        out_specs=(tile, V, V),
+        in_specs=[tile, turned, V, V, weight, V],
+        out_specs=(tile, weight, V, V),
+        scratch_shapes=[pltpu.VMEM((4, TOK, TOK), F32)],
         compiler_params=pltpu.CompilerParams(vmem_limit_bytes=60 << 20),
-    )(tokens, gh, gain, sums, gw, gb)
-    return out, gw, gg[0].reshape(D), gg[1].reshape(D)
+    )(tokens, ghT, gain, sums, gw, gb)
+    return out, gw, gain_sum.reshape(D), bias_sum.reshape(D)
 
 
 def solution(mesh):

time: 146 us -> 136 us (0.932)
  Pallas kernels: 143 us -> 135 us
  local copies, waits for them, and re-layouts: 1.51 us -> 0 us
    pallas_call x1, Pallas kernels: 135 us -> 126 us  [body(): pl.pallas_call(kernel, out_shape=(jax.ShapeDtypeStruct((D, TOK), BF), jax...]
    another operation x1 -> x0, local copies, waits for them, and re-layouts: 1.51 us -> none  [body(): return (out, gw, gg[0].reshape(D), gg[1].reshape(D))]
where the time goes in v3:
time: 136 us
  Pallas kernels  135 us (99%)
    pallas_call x1, Pallas kernels, body(): pl.pallas_call(kernel, out_shape=(jax.ShapeDtypeStruct((D, TOK), BF), jax...  126 us
    pallas_call x1, Pallas kernels, body(): pl.pallas_call(finish, grid=(D // COLS,), out_shape=(jax.ShapeDtypeStruct...  8.63 us

profile of v3, /device:TPU:1, one launch (start us, length us, event | category | flops | bytes accessed | tf_op | source)
XLA Modules:
  0.0 135.7 jit_solution(17366976686432383671)
XLA Ops:
  0.6 126.5 %shard_map.84 = (bf16[14848,128]{1,0:T(8,128)(2,1)}, bf16[928,1024]{1,0:T(8,128)(2,1)}, f32[16,16,128]{2,1,0:T(8,128)}, f32[8,128]{1,0:T(8,128)}) custom-call(bf16[128,14848]{1,0:T(8,128)(2,1)} %x.1, bf16[128,1024]{1,0:T(8,128)(2,1)} %cot.1, bf16[928,1024]{1,0:T(8,128)(2,1)} %w_hbm.1, f32[116,128]{1,0:T(8,128)} %bitcast.4, f32[116,128]{1,0:T(8,128)} %bitcast.6), custom_call_target="tpu_custom_call" | custom-call | tf_op jit(solution)/shard_map/pallas_call | solution.py:473
  127.1 8.6 %shard_map.85 = (bf16[128,14848]{1,0:T(8,128)(2,1)}, bf16[928,1024]{1,0:T(8,128)(2,1)}, f32[116,128]{1,0:T(8,128)}, f32[116,128]{1,0:T(8,128)}) custom-call(bf16[128,14848]{1,0:T(8,128)(2,1)} %x.1, bf16[14848,128]{1,0:T(8,128)(2,1)} %get-tuple-element.12.ghT, f32[116,128]{1,0:T(8,128)} %bitcast.5, f32[8,128]{1,0:T(8,128)} %get-tuple-element.13.sums, ...), custom_call_target="tpu_custom_call" | custom-call | tf_op jit(solution)/shard_map/pallas_call | solution.py:490

commit v4 on v3

--- a/solution.py
+++ b/solution.py
@@ -99,6 +99,14 @@
     own_cot = pltpu.make_async_copy(cot, cots.at[pl.ds(0, TOK)], l_s.at[0])
     own_cot.start()
 
+    pl.semaphore_wait(bar, 2 * (N - 1))
+    cot_copy(jnp.int32(8)).start()
+    cot_copy(jnp.int32(1)).start()
+
+    @pl.loop(1, 4)
+    def _(j):
+        cot_copy(2 * j).start()
+
     x_in.wait()
 
     def turn(t, total):
@@ -109,14 +117,6 @@
 
     total = lax.fori_loop(0, D // 512, turn, jnp.zeros((8, TOK), F32))
     mean = total.sum(0, keepdims=True) / D
-
-    pl.semaphore_wait(bar, 2 * (N - 1))
-    cot_copy(jnp.int32(8)).start()
-    cot_copy(jnp.int32(1)).start()
-
-    @pl.loop(1, 4)
-    def _(j):
-        cot_copy(2 * j).start()
 
     def tok_copy(k, part):
         dev = ahead(k)

time: 136 us -> 136 us (level)
  no operation moved by 1% of the time
where the time goes in v4:
time: 136 us
  Pallas kernels  135 us (99%)
    pallas_call x1, Pallas kernels, body(): pl.pallas_call(kernel, out_shape=(jax.ShapeDtypeStruct((D, TOK), BF), jax...  127 us
    pallas_call x1, Pallas kernels, body(): pl.pallas_call(finish, grid=(D // COLS,), out_shape=(jax.ShapeDtypeStruct...  8.63 us

profile of v4, /device:TPU:1, one launch (start us, length us, event | category | flops | bytes accessed | tf_op | source)
XLA Modules:
  0.0 135.8 jit_solution(18072818117084804595)
XLA Ops:
  0.6 126.6 %shard_map.84 = (bf16[14848,128]{1,0:T(8,128)(2,1)}, bf16[928,1024]{1,0:T(8,128)(2,1)}, f32[16,16,128]{2,1,0:T(8,128)}, f32[8,128]{1,0:T(8,128)}) custom-call(bf16[128,14848]{1,0:T(8,128)(2,1)} %x.1, bf16[128,1024]{1,0:T(8,128)(2,1)} %cot.1, bf16[928,1024]{1,0:T(8,128)(2,1)} %w_hbm.1, f32[116,128]{1,0:T(8,128)} %bitcast.4, f32[116,128]{1,0:T(8,128)} %bitcast.6), custom_call_target="tpu_custom_call" | custom-call | tf_op jit(solution)/shard_map/pallas_call | solution.py:473
  127.2 8.6 %shard_map.85 = (bf16[128,14848]{1,0:T(8,128)(2,1)}, bf16[928,1024]{1,0:T(8,128)(2,1)}, f32[116,128]{1,0:T(8,128)}, f32[116,128]{1,0:T(8,128)}) custom-call(bf16[128,14848]{1,0:T(8,128)(2,1)} %x.1, bf16[14848,128]{1,0:T(8,128)(2,1)} %get-tuple-element.12.ghT, f32[116,128]{1,0:T(8,128)} %bitcast.5, f32[8,128]{1,0:T(8,128)} %get-tuple-element.13.sums, ...), custom_call_target="tpu_custom_call" | custom-call | tf_op jit(solution)/shard_map/pallas_call | solution.py:490
